TPU v7x, 256 devices: a whole 4x4x8 slice. The times are simulated.
256 devices in a mesh: section: 16 (over y_hi, z), blk: 16 (over y_lo, x, core).
Axes of the slice: x: 4, y: 4 (y_hi: 2, y_lo: 2; y = y_hi * 2 + y_lo), z: 8, core: 2. Of those that a mesh axis runs over, the one named last changes fastest.
Arguments:
- waiting: bfloat16 [16, 512, 3072], P('section', 'blk'), may hold values from -12 to 12
- entering: bfloat16 [3, 512, 3072], P(None, 'blk'), may hold values from -12 to 12
- patch_order: int32 [12], replicated, may hold values from 0 to 11, each once
- step_index: int32 [1], replicated, may hold values from 0 to 27
- modulation: float32 [16, 28, 3, 3072], P('section'), may hold values from -4 to 4
- projection: bfloat16 [16, 3072, 3, 2048], P('section', None, None, 'blk'), may hold values from -0.109375 to 0.109375
- key_gain: float32 [16, 2048], P('section', 'blk'), may hold values from 2 to 3
- output_weight: bfloat16 [16, 2048, 3072], P('section', 'blk'), may hold values from -0.125 to 0.125
- stale_keys: bfloat16 [16, 12, 512, 2048], P('section', None, None, 'blk'), may hold values from -4 to 4
- stale_values: bfloat16 [16, 12, 512, 2048], P('section', None, None, 'blk'), may hold values from -4 to 4
Outputs:
- layer_out: bfloat16 [16, 4, 512, 3072], P('section', None, 'blk')
- fresh_kv: bfloat16 [16, 4, 512, 2, 2048], P('section', None, None, None, 'blk')
All inputs are finite; a program needn't handle non-finite values.
Results may differ from a plain program's by a relative error of at most 0.015.
Values may be sent and summed in bfloat16 or wider, within the bound.
No kernel may reach another device: no remote copies, remote signals or barrier semaphores. Data moves between devices by JAX's collectives and lax.ppermute only.
A program may use at most 128 MiB of HBM per device.

v0:
```python
import jax
import jax.numpy as jnp
from jax import lax
from jax.sharding import PartitionSpec as P

D = 3072
HD = 128
PATCHES = 12
TICKS = 4
STEPS = 28
epsilon = 1e-06


def passed_along(x, axis, by):
    size = lax.axis_size(axis)
    pairs = [(i, i + by) for i in range(size) if 0 <= i + by < size]
    return lax.ppermute(x, axis, pairs)


def root_norm(tensor):
    return tensor / jnp.sqrt(jnp.mean(tensor * tensor, axis=-1, keepdims=True) + epsilon)


def one_head(operands):
    head_q, head_k, head_v = operands
    logits = jnp.dot(head_q, head_k.T, preferred_element_type=jnp.float32) * HD ** (-0.5)
    exponent = jnp.exp(logits)
    weights = (exponent / jnp.sum(exponent, axis=-1, keepdims=True)).astype(jnp.bfloat16)
    return jnp.dot(weights, head_v, preferred_element_type=jnp.float32).astype(jnp.bfloat16)


def body(
    waiting,
    entering,
    patch_order,
    step_index,
    modulation,
    projection,
    key_gain,
    output_weight,
    stale_keys,
    stale_values,
):
    section_index = lax.axis_index("section")
    head_cols = projection.shape[3]
    heads_here = head_cols // HD
    selector = (jnp.arange(STEPS, dtype=jnp.int32) == step_index[0]).astype(jnp.float32)
    modulate = jnp.einsum("t,tcd->cd", selector, modulation[0], precision=lax.Precision.HIGHEST)
    flat_weight = projection[0].reshape(D, 3 * head_cols)
    key_scale = key_gain[0].reshape(heads_here, HD)
    out_matrix = output_weight[0]
    cache_k = stale_keys[0]
    cache_v = stale_values[0]
    produced_rows = []
    fresh_rows = []
    current = waiting[0]
    for tick_index in range(TICKS):
        if tick_index == 0:
            inflow = waiting[0]
        else:
            passed = passed_along(current, "section", 1)
            inflow = jnp.where(section_index == 0, entering[tick_index - 1], passed)
        inflow_wide = inflow.astype(jnp.float32)
        normed = (root_norm(inflow_wide) * (1.0 + modulate[1]) + modulate[0]).astype(jnp.bfloat16)
        projected = jnp.dot(
            lax.all_gather(normed, "blk", axis=0, tiled=True),
            flat_weight,
            preferred_element_type=jnp.float32,
        )
        tokens = projected.shape[0]
        projected = projected.reshape(tokens, 3, heads_here, HD)
        queries = root_norm(projected[:, 0]).astype(jnp.bfloat16)
        keys_new = (root_norm(projected[:, 1]) * key_scale).astype(jnp.bfloat16)
        values_new = projected[:, 2].astype(jnp.bfloat16)
        position = jnp.mod(tick_index - section_index, PATCHES)
        patch_slot = lax.dynamic_index_in_dim(patch_order, position, 0, keepdims=False)
        anchor = jnp.zeros((), jnp.int32)
        corner = (patch_slot, anchor, anchor)
        keys_flat = keys_new.reshape(tokens, head_cols)
        values_flat = values_new.reshape(tokens, head_cols)
        cache_k = lax.dynamic_update_slice(cache_k, keys_flat.reshape(1, tokens, head_cols), corner)
        cache_v = lax.dynamic_update_slice(
            cache_v, values_flat.reshape(1, tokens, head_cols), corner
        )
        keys_heads = cache_k.reshape(PATCHES * tokens, heads_here, HD).transpose(1, 0, 2)
        values_heads = cache_v.reshape(PATCHES * tokens, heads_here, HD).transpose(1, 0, 2)
        attended = lax.map(one_head, (queries.transpose(1, 0, 2), keys_heads, values_heads))
        attended = attended.transpose(1, 0, 2).reshape(tokens, head_cols)
        attention = lax.psum_scatter(
            jnp.dot(attended, out_matrix, preferred_element_type=jnp.float32).astype(jnp.bfloat16),
            "blk",
            scatter_dimension=0,
            tiled=True,
        ).astype(jnp.float32)
        current = (inflow_wide + modulate[2] * attention).astype(jnp.bfloat16)
        produced_rows.append(current)
        fresh_rows.append(jnp.stack([keys_flat, values_flat], axis=1))
    layer_out = jnp.stack(produced_rows)[None]
    fresh_kv = jnp.stack(fresh_rows)[None]
    return (layer_out, fresh_kv)


def solution(mesh):
    placed = (
        P("section", "blk", None),
        P(None, "blk", None),
        P(),
        P(),
        P("section", None, None, None),
        P("section", None, None, "blk"),
        P("section", "blk"),
        P("section", "blk", None),
        P("section", None, None, "blk"),
        P("section", None, None, "blk"),
    )
    return jax.shard_map(
        body,
        mesh=mesh,
        in_specs=placed,
        out_specs=(P("section", None, "blk", None), P("section", None, None, None, "blk")),
        check_vma=False,
    )
```

profile of v0, /device:TPU:32, one launch (start us, length us, event | category | flops | bytes accessed | tf_op | source)
XLA Modules:
  0.0 570.3 jit_solution(17247065414648931700)
XLA Ops:
  16.1 35.7 %all-gather.5.cloned.1.call-done = bf16[512,3072]{1,0:T(8,128)(2,1)} async-done(((bf16[32,3072]{1,0:T(8,128)(2,1)}), bf16[512,3072]{1,0:T(8,128)(2,1)}) %all-gather.5.cloned.1.call-update) | async-done | bytes 3145744 | tf_op jit(solution)/shard_map/all_gather | solution.py:66
  51.8 4.5 fusion.14
  56.9 5.7 %fusion = (f32[512]{0:T(512)S(1)}, f32[512,6144]{1,0:T(8,128)}) fusion(bf16[6144,128]{1,0:T(8,128)(2,1)S(1)} %bitcast.227, f32[512]{0:T(512)S(1)} %add_sqrt_fusion.7, f32[512,3,1,128]{3,0,1,2:T(8,128)S(1)} %bitcast.236), kind=kOutput, calls=%fused_computation.8 | convolution fusion | flops 811728384 | bytes 14422016 | tf_op jit(solution)/shard_map/while/body/eval_jaxpr/dot_general | solution.py:26
  62.6 11.0 %convolution_convert_fusion.3 = bf16[512,3072]{1,0:T(8,128)(2,1)} fusion(bf16[6144,128]{1,0:T(8,128)(2,1)} %bitcast.239, f32[512,6144]{1,0:T(8,128)} %get-tuple-element.90, f32[512]{0:T(512)S(1)} %get-tuple-element.89, bf16[1,128,3072]{2,1,0:T(8,128)(2,1)S(1)} %copy-done), kind=kOutput, calls=%fused_computation.19 | convolution fusion | flops 1219035136 | bytes 18089984 | tf_op jit(solution)/shard_map/dot_general | solution.py:90
  73.7 67.9 %reduce-scatter.5.cloned.1.call-done = bf16[32,3072]{1,0:T(8,128)(2,1)} async-done(((bf16[512,3072]{1,0:T(8,128)(2,1)}), bf16[32,3072]{1,0:T(8,128)(2,1)}) %reduce-scatter.5.cloned.1.call-update) | async-done | bytes 196624 | tf_op jit(solution)/shard_map/reduce_scatter | solution.py:89
  146.1 4.2 collective-permute-done
  155.2 36.0 %all-gather.7.cloned.1.call-done = bf16[512,3072]{1,0:T(8,128)(2,1)} async-done(((bf16[32,3072]{1,0:T(8,128)(2,1)}), bf16[512,3072]{1,0:T(8,128)(2,1)}) %all-gather.7.cloned.1.call-update) | async-done | bytes 3145744 | tf_op jit(solution)/shard_map/all_gather | solution.py:66
  191.3 4.5 fusion.20
  196.7 6.3 %fusion.1 = (f32[512]{0:T(512)}, f32[512,6144]{1,0:T(8,128)}) fusion(bf16[6144,128]{1,0:T(8,128)(2,1)S(1)} %bitcast.228, f32[512]{0:T(512)S(1)} %add_sqrt_fusion.5, f32[512,3,1,128]{3,0,2,1:T(8,128)S(1)} %fusion.20), kind=kOutput, calls=%fused_computation.9 | convolution fusion | flops 811728384 | bytes 14422016 | tf_op jit(solution)/shard_map/while/body/eval_jaxpr/dot_general | solution.py:26
  203.0 11.0 %convolution_convert_fusion.2 = bf16[512,3072]{1,0:T(8,128)(2,1)} fusion(bf16[6144,128]{1,0:T(8,128)(2,1)} %bitcast.240, f32[512,6144]{1,0:T(8,128)} %get-tuple-element.92, f32[512]{0:T(512)} %get-tuple-element.91, bf16[1,128,3072]{2,1,0:T(8,128)(2,1)S(1)} %copy-done), kind=kOutput, calls=%fused_computation.18 | convolution fusion | flops 1219035136 | bytes 18089984 | tf_op jit(solution)/shard_map/dot_general | solution.py:90
  214.1 67.9 %reduce-scatter.7.cloned.1.call-done = bf16[32,3072]{1,0:T(8,128)(2,1)} async-done(((bf16[512,3072]{1,0:T(8,128)(2,1)}), bf16[32,3072]{1,0:T(8,128)(2,1)}) %reduce-scatter.7.cloned.1.call-update) | async-done | bytes 196624 | tf_op jit(solution)/shard_map/reduce_scatter | solution.py:89
  283.0 3.5 collective-permute-start.1
  286.5 4.1 collective-permute-done.1
  295.6 35.9 %all-gather.9.cloned.1.call-done = bf16[512,3072]{1,0:T(8,128)(2,1)} async-done(((bf16[32,3072]{1,0:T(8,128)(2,1)}), bf16[512,3072]{1,0:T(8,128)(2,1)}) %all-gather.9.cloned.1.call-update) | async-done | bytes 3145744 | tf_op jit(solution)/shard_map/all_gather | solution.py:66
  331.5 4.5 fusion.25
  336.9 6.3 %fusion.2 = (f32[512]{0:T(512)}, f32[512,6144]{1,0:T(8,128)}) fusion(bf16[6144,128]{1,0:T(8,128)(2,1)S(1)} %bitcast.229, f32[512]{0:T(512)S(1)} %add_sqrt_fusion.3, f32[512,3,1,128]{3,0,2,1:T(8,128)S(1)} %fusion.25), kind=kOutput, calls=%fused_computation.10 | convolution fusion | flops 811728384 | bytes 14422016 | tf_op jit(solution)/shard_map/while/body/eval_jaxpr/dot_general | solution.py:26
  343.2 11.0 %convolution_convert_fusion.1 = bf16[512,3072]{1,0:T(8,128)(2,1)} fusion(bf16[6144,128]{1,0:T(8,128)(2,1)} %bitcast.241, f32[512,6144]{1,0:T(8,128)} %get-tuple-element.94, f32[512]{0:T(512)} %get-tuple-element.93, bf16[1,128,3072]{2,1,0:T(8,128)(2,1)S(1)} %copy-done), kind=kOutput, calls=%fused_computation.17 | convolution fusion | flops 1219035136 | bytes 18089984 | tf_op jit(solution)/shard_map/dot_general | solution.py:90
  354.3 67.9 %reduce-scatter.9.cloned.1.call-done = bf16[32,3072]{1,0:T(8,128)(2,1)} async-done(((bf16[512,3072]{1,0:T(8,128)(2,1)}), bf16[32,3072]{1,0:T(8,128)(2,1)}) %reduce-scatter.9.cloned.1.call-update) | async-done | bytes 196624 | tf_op jit(solution)/shard_map/reduce_scatter | solution.py:89
  426.7 4.1 collective-permute-done.2
  435.5 36.1 %all-gather.11.cloned.1.call-done = bf16[512,3072]{1,0:T(8,128)(2,1)} async-done(((bf16[32,3072]{1,0:T(8,128)(2,1)}), bf16[512,3072]{1,0:T(8,128)(2,1)}) %all-gather.11.cloned.1.call-update) | async-done | bytes 3145744 | tf_op jit(solution)/shard_map/all_gather | solution.py:66
  471.7 4.5 fusion.30
  476.7 5.7 %fusion.3 = (f32[512]{0:T(512)S(1)}, f32[512,6144]{1,0:T(8,128)}) fusion(bf16[6144,128]{1,0:T(8,128)(2,1)S(1)} %bitcast.230, f32[512]{0:T(512)S(1)} %add_sqrt_fusion.1, f32[512,3,1,128]{3,0,2,1:T(8,128)S(1)} %fusion.30), kind=kOutput, calls=%fused_computation.11 | convolution fusion | flops 811728384 | bytes 14422016 | tf_op jit(solution)/shard_map/while/body/eval_jaxpr/dot_general | solution.py:26
  482.5 11.0 %convolution_convert_fusion = bf16[512,3072]{1,0:T(8,128)(2,1)} fusion(bf16[6144,128]{1,0:T(8,128)(2,1)} %bitcast.242, f32[512,6144]{1,0:T(8,128)} %get-tuple-element.96, f32[512]{0:T(512)S(1)} %get-tuple-element.95, bf16[1,128,3072]{2,1,0:T(8,128)(2,1)S(1)} %copy-done), kind=kOutput, calls=%fused_computation.16 | convolution fusion | flops 1219035136 | bytes 18089984 | tf_op jit(solution)/shard_map/dot_general | solution.py:90
  499.5 62.0 %reduce-scatter.11.cloned.1.call-done = bf16[32,3072]{1,0:T(8,128)(2,1)} async-done(((bf16[512,3072]{1,0:T(8,128)(2,1)}), bf16[32,3072]{1,0:T(8,128)(2,1)}) %reduce-scatter.11.cloned.1.call-update) | async-done | bytes 196624 | tf_op jit(solution)/shard_map/reduce_scatter | solution.py:89
  (137 shorter events, 35.6 us)
Async XLA Ops:
  7.2 55.5 %copy-start = (bf16[1,128,3072]{2,1,0:T(8,128)(2,1)S(1)}, bf16[1,128,3072]{2,1,0:T(8,128)(2,1)}, u32[]{:S(2)}) copy-start(bf16[1,128,3072]{2,1,0:T(8,128)(2,1)} %param.17) | copy-start | bytes 2359300
  7.2 44.6 %all-gather.5.cloned.1.call-start = ((), (), s32[]{:S(2)}) async-start(), calls=%async_computation.4 | async-start | bytes 3342336 | tf_op jit(solution)/shard_map/all_gather | solution.py:66
  9.8 46.6 %copy-start.22 = (f32[1,3072]{1,0:T(1,128)}, f32[1,3072]{1,0:T(1,128)S(1)}, u32[]{:S(2)}) copy-start(f32[1,3072]{1,0:T(1,128)S(1)} %get-tuple-element.80) | copy-start | bytes 36868
  10.8 130.8 %reduce-scatter.5.cloned.1.call-start = ((), (), s32[]{:S(2)}) async-start(), calls=%async_computation.5 | async-start | bytes 3342336 | tf_op jit(solution)/shard_map/reduce_scatter | solution.py:89
  16.0 40.7 %copy-start.1 = (bf16[1,12,512,128]{3,2,1,0:T(8,128)(2,1)S(1)}, bf16[1,12,512,128]{3,2,1,0:T(8,128)(2,1)}, u32[]{:S(2)}) copy-start(bf16[1,12,512,128]{3,2,1,0:T(8,128)(2,1)} %param.18) | copy-start | bytes 4718596
  16.0 40.7 %copy-start.28 = (f32[1,128]{1,0:T(1,128)S(1)}, f32[1,128]{1,0:T(1,128)}, u32[]{:S(2)}) copy-start(f32[1,128]{1,0:T(1,128)} %param.16) | copy-start | bytes 1540
  73.6 117.6 %all-gather.7.cloned.1.call-start = ((), (), s32[]{:S(2)}) async-start(), calls=%async_computation.6 | async-start | bytes 3342336 | tf_op jit(solution)/shard_map/all_gather | solution.py:66
  142.6 7.7 %collective-permute-start = (bf16[32,3072]{1,0:T(8,128)(2,1)S(1)}, bf16[32,3072]{1,0:T(8,128)(2,1)}, u32[]{:S(2)}, u32[]{:S(2)}) collective-permute-start(bf16[32,3072]{1,0:T(8,128)(2,1)S(1)} %fusion.65), channel_id=1, source_target_pairs={{0,16},{16,32},{32,48},{48,64},{64,80},{80,96},{96,112},{112,128},... | collective-permute-start | bytes 589832 | tf_op jit(solution)/shard_map/ppermute | solution.py:17
  153.1 129.0 %reduce-scatter.7.cloned.1.call-start = ((), (), s32[]{:S(2)}) async-start(), calls=%async_computation.7 | async-start | bytes 3342336 | tf_op jit(solution)/shard_map/reduce_scatter | solution.py:89
  195.8 7.2 %copy-start.2 = (f32[512,3,1,128]{3,0,2,1:T(8,128)}, f32[512,3,1,128]{3,0,2,1:T(8,128)S(1)}, u32[]{:S(2)}) copy-start(f32[512,3,1,128]{3,0,2,1:T(8,128)S(1)} %fusion.20) | copy-start | bytes 2359300
  196.7 6.3 %copy-start.11 = (bf16[12,512,128]{2,1,0:T(8,128)(2,1)}, bf16[12,512,128]{2,1,0:T(8,128)(2,1)S(1)}, u32[]{:S(2)}) copy-start(bf16[12,512,128]{2,1,0:T(8,128)(2,1)S(1)} %get-tuple-element.72) | copy-start | bytes 4718596
  214.0 117.4 %all-gather.9.cloned.1.call-start = ((), (), s32[]{:S(2)}) async-start(), calls=%async_computation.8 | async-start | bytes 3342336 | tf_op jit(solution)/shard_map/all_gather | solution.py:66
  283.0 7.6 %collective-permute-start.1 = (bf16[32,3072]{1,0:T(8,128)(2,1)S(1)}, bf16[32,3072]{1,0:T(8,128)(2,1)S(1)}, u32[]{:S(2)}, u32[]{:S(2)}) collective-permute-start(bf16[32,3072]{1,0:T(8,128)(2,1)S(1)} %fusion.50), channel_id=1, source_target_pairs={{0,16},{16,32},{32,48},{48,64},{64,80},{80,96},{96,112},{112,128},... | collective-permute-start | bytes 589832 | tf_op jit(solution)/shard_map/ppermute | solution.py:17
  293.3 129.0 %reduce-scatter.9.cloned.1.call-start = ((), (), s32[]{:S(2)}) async-start(), calls=%async_computation.9 | async-start | bytes 3342336 | tf_op jit(solution)/shard_map/reduce_scatter | solution.py:89
  336.0 7.2 %copy-start.4 = (f32[512,3,1,128]{3,0,2,1:T(8,128)}, f32[512,3,1,128]{3,0,2,1:T(8,128)S(1)}, u32[]{:S(2)}) copy-start(f32[512,3,1,128]{3,0,2,1:T(8,128)S(1)} %fusion.25) | copy-start | bytes 2359300
  336.9 6.3 %copy-start.13 = (bf16[12,512,128]{2,1,0:T(8,128)(2,1)}, bf16[12,512,128]{2,1,0:T(8,128)(2,1)S(1)}, u32[]{:S(2)}) copy-start(bf16[12,512,128]{2,1,0:T(8,128)(2,1)S(1)} %get-tuple-element.70) | copy-start | bytes 4718596
  354.2 117.4 %all-gather.11.cloned.1.call-start = ((), (), s32[]{:S(2)}) async-start(), calls=%async_computation.10 | async-start | bytes 3342336 | tf_op jit(solution)/shard_map/all_gather | solution.py:66
  423.2 7.6 %collective-permute-start.2 = (bf16[32,3072]{1,0:T(8,128)(2,1)S(1)}, bf16[32,3072]{1,0:T(8,128)(2,1)S(1)}, u32[]{:S(2)}, u32[]{:S(2)}) collective-permute-start(bf16[32,3072]{1,0:T(8,128)(2,1)S(1)} %fusion.55), channel_id=1, source_target_pairs={{0,16},{16,32},{32,48},{48,64},{64,80},{80,96},{96,112},{112,128},... | collective-permute-start | bytes 589832 | tf_op jit(solution)/shard_map/ppermute | solution.py:17
  433.5 128.0 %reduce-scatter.11.cloned.1.call-start = ((), (), s32[]{:S(2)}) async-start(), calls=%async_computation.11 | async-start | bytes 3342336 | tf_op jit(solution)/shard_map/reduce_scatter | solution.py:89
  435.5 41.0 %copy-start.31 = (f32[1,128]{1,0:T(1,128)S(1)}, f32[1,128]{1,0:T(1,128)}, u32[]{:S(2)}) copy-start(f32[1,128]{1,0:T(1,128)} %param.16) | copy-start | bytes 1540
  476.2 6.3 %copy-start.6 = (f32[512,3,1,128]{3,0,2,1:T(8,128)}, f32[512,3,1,128]{3,0,2,1:T(8,128)S(1)}, u32[]{:S(2)}) copy-start(f32[512,3,1,128]{3,0,2,1:T(8,128)S(1)} %fusion.30) | copy-start | bytes 2359300
  497.1 64.3 %copy-start.23 = (f32[1,3072]{1,0:T(1,128)S(1)}, f32[1,3072]{1,0:T(1,128)}, u32[]{:S(2)}) copy-start(f32[1,3072]{1,0:T(1,128)} %get-tuple-element.73) | copy-start | bytes 36868
  497.2 65.3 %copy-start.19 = (bf16[32,3072]{1,0:T(8,128)(2,1)S(1)}, bf16[32,3072]{1,0:T(8,128)(2,1)}, u32[]{:S(2)}) copy-start(bf16[32,3072]{1,0:T(8,128)(2,1)} %copy-done.18) | copy-start | bytes 589828
  497.2 65.3 %copy-start.21 = (bf16[32,3072]{1,0:T(8,128)(2,1)S(1)}, bf16[32,3072]{1,0:T(8,128)(2,1)}, u32[]{:S(2)}) copy-start(bf16[32,3072]{1,0:T(8,128)(2,1)} %copy-done.20) | copy-start | bytes 589828
  (20 other events, 69.5 us)
Sparse Core Ops, SparseCore 0:
  10.9 40.8 all-gather.4
  73.8 67.8 reduce-scatter.4
  153.2 38.0 all-gather.6
  214.2 67.8 reduce-scatter.6
  293.4 38.0 all-gather.8
  354.4 67.8 reduce-scatter.8
  433.6 38.0 all-gather.10
  493.6 67.8 reduce-scatter.10
where the time goes:
time: 571 us; the launch traced here: 570 us
  waiting for transfers between devices  422 us (74%)
  matrix products  86.7 us (15%)
  between operations  23.2 us (4%)
  other arithmetic  18.1 us (3%)
  starting transfers between devices  11.4 us (2%)
  local copies, waits for them, and re-layouts  8.91 us (2%)
    reduce_scatter x4, waiting for transfers between devices, body(): lax.psum_scatter(jnp.dot(attended, out_matrix, preferred_element_type=jnp...  266 us
    all_gather x4, waiting for transfers between devices, body(): lax.all_gather(normed, 'blk', axis=0, tiled=True)  144 us
    dot_general x4, matrix products, body(): jnp.dot(attended, out_matrix, preferred_element_type=jnp.float32)  43.9 us
    dot_general x4, matrix products, one_head(): jnp.dot(head_q, head_k.T, preferred_element_type=jnp.float32) * HD ** (-0.5)  24 us
    dot_general x4, matrix products, body(): jnp.dot(lax.all_gather(normed, 'blk', axis=0, tiled=True), flat_weight, p...  18.1 us
    ppermute x3, waiting for transfers between devices, passed_along(): return lax.ppermute(x, axis, pairs)  12.4 us
  transfers between devices with their start and end apart: 11, of which 11 were waited for; matrix products, arithmetic and copies ran while one was open for 1% of the time, Pallas kernels for 0%

commit v1 on v0

--- a/solution.py
+++ b/solution.py
@@ -63,7 +63,9 @@
         inflow_wide = inflow.astype(jnp.float32)
         normed = (root_norm(inflow_wide) * (1.0 + modulate[1]) + modulate[0]).astype(jnp.bfloat16)
         projected = jnp.dot(
-            lax.all_gather(normed, "blk", axis=0, tiled=True),
+            jnp.concatenate(
+                lax.all_to_all(jnp.stack([normed] * lax.axis_size("blk")), "blk", 0, 0), axis=0
+            ),
             flat_weight,
             preferred_element_type=jnp.float32,
         )

time: 571 us -> 615 us (1.077)
  waiting for transfers between devices: 422 us -> 441 us
  starting transfers between devices: 11.4 us -> 30.3 us
  local copies, waits for them, and re-layouts: 8.91 us -> 17.2 us
    all_to_all x0 -> x4, waiting for transfers between devices: none -> 157 us  [body(): lax.all_to_all(jnp.stack([normed] * lax.axis_size('blk')), 'blk', 0, 0)]
    all_gather x4 -> x0, waiting for transfers between devices: 144 us -> none  [body(): lax.all_gather(normed, 'blk', axis=0, tiled=True)]
    all_to_all x0 -> x4, starting transfers between devices: none -> 19 us  [body(): lax.all_to_all(jnp.stack([normed] * lax.axis_size('blk')), 'blk', 0, 0)]
    another operation x0 -> x4, local copies, waits for them, and re-layouts: none -> 8.26 us  [body(): jnp.stack([normed] * lax.axis_size('blk'))]
where the time goes in v1:
time: 615 us; the launch traced here: 614 us
  waiting for transfers between devices  441 us (72%)
  matrix products  86.6 us (14%)
  starting transfers between devices  30.3 us (5%)
  between operations  22.8 us (4%)
  local copies, waits for them, and re-layouts  17.2 us (3%)
  other arithmetic  15.4 us (3%)
    reduce_scatter x4, waiting for transfers between devices, body(): lax.psum_scatter(jnp.dot(attended, out_matrix, preferred_element_type=jnp...  272 us
    all_to_all x4, waiting for transfers between devices, body(): lax.all_to_all(jnp.stack([normed] * lax.axis_size('blk')), 'blk', 0, 0)  157 us
    dot_general x4, matrix products, body(): jnp.dot(attended, out_matrix, preferred_element_type=jnp.float32)  43.9 us
    dot_general x4, matrix products, one_head(): jnp.dot(head_q, head_k.T, preferred_element_type=jnp.float32) * HD ** (-0.5)  24 us
    all_to_all x4, starting transfers between devices, body(): lax.all_to_all(jnp.stack([normed] * lax.axis_size('blk')), 'blk', 0, 0)  19 us
    dot_general x4, matrix products, body(): jnp.dot(jnp.concatenate(lax.all_to_all(jnp.stack([normed] * lax.axis_size...  18.2 us
    ppermute x3, waiting for transfers between devices, passed_along(): return lax.ppermute(x, axis, pairs)  12.4 us
  transfers between devices with their start and end apart: 11, of which 11 were waited for; matrix products, arithmetic and copies ran while one was open for 1% of the time, Pallas kernels for 0%

profile of v1, /device:TPU:32, one launch (start us, length us, event | category | flops | bytes accessed | tf_op | source)
XLA Modules:
  0.0 613.7 jit_solution(9949643212134116306)
XLA Ops:
  12.1 5.6 all-to-all-start
  23.1 37.0 %all-to-all-done = bf16[16,32,3072]{2,1,0:T(8,128)(2,1)} async-done(((bf16[16,32,3072]{2,1,0:T(8,128)(2,1)}), bf16[16,32,3072]{2,1,0:T(8,128)(2,1)}, u32[]{:S(2)}, u32[]{:S(2)}) %all-to-all-start) | async-done | bytes 3145760 | tf_op jit(solution)/shard_map/all_to_all | solution.py:67
  60.2 4.6 fusion.14
  65.3 5.7 fusion
  71.0 11.0 %convolution_convert_fusion.3 = bf16[512,3072]{1,0:T(8,128)(2,1)} fusion(bf16[6144,128]{1,0:T(8,128)(2,1)} %bitcast.244, f32[512,6144]{1,0:T(8,128)} %get-tuple-element.90, f32[512]{0:T(512)S(1)} %get-tuple-element.89, bf16[1,128,3072]{2,1,0:T(8,128)(2,1)S(1)} %copy-done), kind=kOutput, calls=%fused_computation.19 | convolution fusion | flops 1219035136 | bytes 18089984 | tf_op jit(solution)/shard_map/dot_general | solution.py:92
  82.0 69.5 %reduce-scatter.5.cloned.1.call-done = bf16[32,3072]{1,0:T(8,128)(2,1)} async-done(((bf16[512,3072]{1,0:T(8,128)(2,1)}), bf16[32,3072]{1,0:T(8,128)(2,1)}) %reduce-scatter.5.cloned.1.call-update) | async-done | bytes 196624 | tf_op jit(solution)/shard_map/reduce_scatter | solution.py:91
  164.3 4.5 all-to-all-start.1
  171.0 40.0 %all-to-all-done.1 = bf16[16,32,3072]{2,1,0:T(8,128)(2,1)} async-done(((bf16[16,32,3072]{2,1,0:T(8,128)(2,1)}), bf16[16,32,3072]{2,1,0:T(8,128)(2,1)}, u32[]{:S(2)}, u32[]{:S(2)}) %all-to-all-start.1) | async-done | bytes 3145760 | tf_op jit(solution)/shard_map/all_to_all | solution.py:67
  211.0 4.5 fusion.16
  216.5 6.3 %fusion.1 = (f32[512]{0:T(512)}, f32[512,6144]{1,0:T(8,128)}) fusion(bf16[6144,128]{1,0:T(8,128)(2,1)S(1)} %bitcast.233, f32[512]{0:T(512)S(1)} %add_sqrt_fusion.5, f32[512,3,1,128]{3,0,2,1:T(8,128)S(1)} %fusion.16), kind=kOutput, calls=%fused_computation.9 | convolution fusion | flops 811728384 | bytes 14422016 | tf_op jit(solution)/shard_map/while/body/eval_jaxpr/dot_general | solution.py:26
  222.8 11.0 %convolution_convert_fusion.2 = bf16[512,3072]{1,0:T(8,128)(2,1)} fusion(bf16[6144,128]{1,0:T(8,128)(2,1)} %bitcast.245, f32[512,6144]{1,0:T(8,128)} %get-tuple-element.92, f32[512]{0:T(512)} %get-tuple-element.91, bf16[1,128,3072]{2,1,0:T(8,128)(2,1)S(1)} %copy-done), kind=kOutput, calls=%fused_computation.18 | convolution fusion | flops 1219035136 | bytes 18089984 | tf_op jit(solution)/shard_map/dot_general | solution.py:92
  233.8 69.4 %reduce-scatter.7.cloned.1.call-done = bf16[32,3072]{1,0:T(8,128)(2,1)} async-done(((bf16[512,3072]{1,0:T(8,128)(2,1)}), bf16[32,3072]{1,0:T(8,128)(2,1)}) %reduce-scatter.7.cloned.1.call-update) | async-done | bytes 196624 | tf_op jit(solution)/shard_map/reduce_scatter | solution.py:91
  315.8 4.5 all-to-all-start.2
  322.3 40.2 %all-to-all-done.2 = bf16[16,32,3072]{2,1,0:T(8,128)(2,1)} async-done(((bf16[16,32,3072]{2,1,0:T(8,128)(2,1)}), bf16[16,32,3072]{2,1,0:T(8,128)(2,1)}, u32[]{:S(2)}, u32[]{:S(2)}) %all-to-all-start.2) | async-done | bytes 3145760 | tf_op jit(solution)/shard_map/all_to_all | solution.py:67
  362.5 4.5 fusion.19
  368.0 6.3 %fusion.2 = (f32[512]{0:T(512)}, f32[512,6144]{1,0:T(8,128)}) fusion(bf16[6144,128]{1,0:T(8,128)(2,1)S(1)} %bitcast.234, f32[512]{0:T(512)S(1)} %add_sqrt_fusion.3, f32[512,3,1,128]{3,0,2,1:T(8,128)S(1)} %fusion.19), kind=kOutput, calls=%fused_computation.10 | convolution fusion | flops 811728384 | bytes 14422016 | tf_op jit(solution)/shard_map/while/body/eval_jaxpr/dot_general | solution.py:26
  374.3 11.0 %convolution_convert_fusion.1 = bf16[512,3072]{1,0:T(8,128)(2,1)} fusion(bf16[6144,128]{1,0:T(8,128)(2,1)} %bitcast.246, f32[512,6144]{1,0:T(8,128)} %get-tuple-element.94, f32[512]{0:T(512)} %get-tuple-element.93, bf16[1,128,3072]{2,1,0:T(8,128)(2,1)S(1)} %copy-done), kind=kOutput, calls=%fused_computation.17 | convolution fusion | flops 1219035136 | bytes 18089984 | tf_op jit(solution)/shard_map/dot_general | solution.py:92
  385.3 69.4 %reduce-scatter.9.cloned.1.call-done = bf16[32,3072]{1,0:T(8,128)(2,1)} async-done(((bf16[512,3072]{1,0:T(8,128)(2,1)}), bf16[32,3072]{1,0:T(8,128)(2,1)}) %reduce-scatter.9.cloned.1.call-update) | async-done | bytes 196624 | tf_op jit(solution)/shard_map/reduce_scatter | solution.py:91
  467.3 4.5 all-to-all-start.3
  473.9 40.0 %all-to-all-done.3 = bf16[16,32,3072]{2,1,0:T(8,128)(2,1)} async-done(((bf16[16,32,3072]{2,1,0:T(8,128)(2,1)}), bf16[16,32,3072]{2,1,0:T(8,128)(2,1)}, u32[]{:S(2)}, u32[]{:S(2)}) %all-to-all-start.3) | async-done | bytes 3145760 | tf_op jit(solution)/shard_map/all_to_all | solution.py:67
  514.0 4.5 fusion.22
  519.1 5.7 fusion.3
  524.8 11.0 %convolution_convert_fusion = bf16[512,3072]{1,0:T(8,128)(2,1)} fusion(bf16[6144,128]{1,0:T(8,128)(2,1)} %bitcast.247, f32[512,6144]{1,0:T(8,128)} %get-tuple-element.96, f32[512]{0:T(512)S(1)} %get-tuple-element.95, bf16[1,128,3072]{2,1,0:T(8,128)(2,1)S(1)} %copy-done), kind=kOutput, calls=%fused_computation.16 | convolution fusion | flops 1219035136 | bytes 18089984 | tf_op jit(solution)/shard_map/dot_general | solution.py:92
  541.8 63.4 %reduce-scatter.11.cloned.1.call-done = bf16[32,3072]{1,0:T(8,128)(2,1)} async-done(((bf16[512,3072]{1,0:T(8,128)(2,1)}), bf16[32,3072]{1,0:T(8,128)(2,1)}) %reduce-scatter.11.cloned.1.call-update) | async-done | bytes 196624 | tf_op jit(solution)/shard_map/reduce_scatter | solution.py:91
  (137 shorter events, 56.8 us)
Async XLA Ops:
  7.2 63.8 %copy-start = (bf16[1,128,3072]{2,1,0:T(8,128)(2,1)S(1)}, bf16[1,128,3072]{2,1,0:T(8,128)(2,1)}, u32[]{:S(2)}) copy-start(bf16[1,128,3072]{2,1,0:T(8,128)(2,1)} %param.17) | copy-start | bytes 2359300
  12.1 7.8 %copy-start.7 = (bf16[1,3072,3,128]{3,1,2,0:T(8,128)(2,1)S(1)}, bf16[1,3072,3,128]{3,1,2,0:T(8,128)(2,1)}, u32[]{:S(2)}) copy-start(bf16[1,3072,3,128]{3,1,2,0:T(8,128)(2,1)} %param.15) | copy-start | bytes 7077892
  12.1 48.0 %all-to-all-start = ((bf16[16,32,3072]{2,1,0:T(8,128)(2,1)}), bf16[16,32,3072]{2,1,0:T(8,128)(2,1)}, u32[]{:S(2)}, u32[]{:S(2)}) async-start(bf16[16,32,3072]{2,1,0:T(8,128)(2,1)} %stack.39), calls=%async_computation | async-start | bytes 6291456 | tf_op jit(solution)/shard_map/all_to_all | solution.py:67
  17.7 133.8 %reduce-scatter.5.cloned.1.call-start = ((), (), s32[]{:S(2)}) async-start(), calls=%async_computation.8 | async-start | bytes 3342336 | tf_op jit(solution)/shard_map/reduce_scatter | solution.py:91
  152.5 7.7 %collective-permute-start = (bf16[32,3072]{1,0:T(8,128)(2,1)S(1)}, bf16[32,3072]{1,0:T(8,128)(2,1)}, u32[]{:S(2)}, u32[]{:S(2)}) collective-permute-start(bf16[32,3072]{1,0:T(8,128)(2,1)S(1)} %fusion.39), channel_id=1, source_target_pairs={{0,16},{16,32},{32,48},{48,64},{64,80},{80,96},{96,112},{112,128},... | collective-permute-start | bytes 589832 | tf_op jit(solution)/shard_map/ppermute | solution.py:17
  164.3 46.7 %all-to-all-start.1 = ((bf16[16,32,3072]{2,1,0:T(8,128)(2,1)}), bf16[16,32,3072]{2,1,0:T(8,128)(2,1)}, u32[]{:S(2)}, u32[]{:S(2)}) async-start(bf16[16,32,3072]{2,1,0:T(8,128)(2,1)} %stack.41), calls=%async_computation.2 | async-start | bytes 6291456 | tf_op jit(solution)/shard_map/all_to_all | solution.py:67
  168.8 134.4 %reduce-scatter.7.cloned.1.call-start = ((), (), s32[]{:S(2)}) async-start(), calls=%async_computation.9 | async-start | bytes 3342336 | tf_op jit(solution)/shard_map/reduce_scatter | solution.py:91
  215.6 7.2 %copy-start.2 = (f32[512,3,1,128]{3,0,2,1:T(8,128)}, f32[512,3,1,128]{3,0,2,1:T(8,128)S(1)}, u32[]{:S(2)}) copy-start(f32[512,3,1,128]{3,0,2,1:T(8,128)S(1)} %fusion.16) | copy-start | bytes 2359300
  216.5 6.3 %copy-start.11 = (bf16[12,512,128]{2,1,0:T(8,128)(2,1)}, bf16[12,512,128]{2,1,0:T(8,128)(2,1)S(1)}, u32[]{:S(2)}) copy-start(bf16[12,512,128]{2,1,0:T(8,128)(2,1)S(1)} %get-tuple-element.72) | copy-start | bytes 4718596
  304.2 8.7 %copy-start.18 = (bf16[32,3072]{1,0:T(8,128)(2,1)}, bf16[32,3072]{1,0:T(8,128)(2,1)S(1)}, u32[]{:S(2)}) copy-start(bf16[32,3072]{1,0:T(8,128)(2,1)S(1)} %fusion.47) | copy-start | bytes 589828
  304.2 7.6 %collective-permute-start.1 = (bf16[32,3072]{1,0:T(8,128)(2,1)S(1)}, bf16[32,3072]{1,0:T(8,128)(2,1)S(1)}, u32[]{:S(2)}, u32[]{:S(2)}) collective-permute-start(bf16[32,3072]{1,0:T(8,128)(2,1)S(1)} %fusion.47), channel_id=1, source_target_pairs={{0,16},{16,32},{32,48},{48,64},{64,80},{80,96},{96,112},{112,128},... | collective-permute-start | bytes 589832 | tf_op jit(solution)/shard_map/ppermute | solution.py:17
  315.8 46.7 %all-to-all-start.2 = ((bf16[16,32,3072]{2,1,0:T(8,128)(2,1)}), bf16[16,32,3072]{2,1,0:T(8,128)(2,1)}, u32[]{:S(2)}, u32[]{:S(2)}) async-start(bf16[16,32,3072]{2,1,0:T(8,128)(2,1)} %stack.43), calls=%async_computation.4 | async-start | bytes 6291456 | tf_op jit(solution)/shard_map/all_to_all | solution.py:67
  320.3 134.4 %reduce-scatter.9.cloned.1.call-start = ((), (), s32[]{:S(2)}) async-start(), calls=%async_computation.10 | async-start | bytes 3342336 | tf_op jit(solution)/shard_map/reduce_scatter | solution.py:91
  367.1 7.2 %copy-start.4 = (f32[512,3,1,128]{3,0,2,1:T(8,128)}, f32[512,3,1,128]{3,0,2,1:T(8,128)S(1)}, u32[]{:S(2)}) copy-start(f32[512,3,1,128]{3,0,2,1:T(8,128)S(1)} %fusion.19) | copy-start | bytes 2359300
  368.0 6.3 %copy-start.13 = (bf16[12,512,128]{2,1,0:T(8,128)(2,1)}, bf16[12,512,128]{2,1,0:T(8,128)(2,1)S(1)}, u32[]{:S(2)}) copy-start(bf16[12,512,128]{2,1,0:T(8,128)(2,1)S(1)} %get-tuple-element.70) | copy-start | bytes 4718596
  455.7 8.7 %copy-start.20 = (bf16[32,3072]{1,0:T(8,128)(2,1)}, bf16[32,3072]{1,0:T(8,128)(2,1)S(1)}, u32[]{:S(2)}) copy-start(bf16[32,3072]{1,0:T(8,128)(2,1)S(1)} %fusion.52) | copy-start | bytes 589828
  455.7 7.6 %collective-permute-start.2 = (bf16[32,3072]{1,0:T(8,128)(2,1)S(1)}, bf16[32,3072]{1,0:T(8,128)(2,1)S(1)}, u32[]{:S(2)}, u32[]{:S(2)}) collective-permute-start(bf16[32,3072]{1,0:T(8,128)(2,1)S(1)} %fusion.52), channel_id=1, source_target_pairs={{0,16},{16,32},{32,48},{48,64},{64,80},{80,96},{96,112},{112,128},... | collective-permute-start | bytes 589832 | tf_op jit(solution)/shard_map/ppermute | solution.py:17
  467.3 46.7 %all-to-all-start.3 = ((bf16[16,32,3072]{2,1,0:T(8,128)(2,1)}), bf16[16,32,3072]{2,1,0:T(8,128)(2,1)}, u32[]{:S(2)}, u32[]{:S(2)}) async-start(bf16[16,32,3072]{2,1,0:T(8,128)(2,1)} %stack.45), calls=%async_computation.6 | async-start | bytes 6291456 | tf_op jit(solution)/shard_map/all_to_all | solution.py:67
  471.8 133.4 %reduce-scatter.11.cloned.1.call-start = ((), (), s32[]{:S(2)}) async-start(), calls=%async_computation.11 | async-start | bytes 3342336 | tf_op jit(solution)/shard_map/reduce_scatter | solution.py:91
  518.5 6.3 %copy-start.6 = (f32[512,3,1,128]{3,0,2,1:T(8,128)}, f32[512,3,1,128]{3,0,2,1:T(8,128)S(1)}, u32[]{:S(2)}) copy-start(f32[512,3,1,128]{3,0,2,1:T(8,128)S(1)} %fusion.22) | copy-start | bytes 2359300
  519.1 5.7 copy-start.15
  539.5 65.7 %copy-start.23 = (f32[1,3072]{1,0:T(1,128)S(1)}, f32[1,3072]{1,0:T(1,128)}, u32[]{:S(2)}) copy-start(f32[1,3072]{1,0:T(1,128)} %get-tuple-element.73) | copy-start | bytes 36868
  539.5 66.7 %copy-start.19 = (bf16[32,3072]{1,0:T(8,128)(2,1)S(1)}, bf16[32,3072]{1,0:T(8,128)(2,1)}, u32[]{:S(2)}) copy-start(bf16[32,3072]{1,0:T(8,128)(2,1)} %copy-done.18) | copy-start | bytes 589828
  539.5 66.7 %copy-start.21 = (bf16[32,3072]{1,0:T(8,128)(2,1)S(1)}, bf16[32,3072]{1,0:T(8,128)(2,1)}, u32[]{:S(2)}) copy-start(bf16[32,3072]{1,0:T(8,128)(2,1)} %copy-done.20) | copy-start | bytes 589828
  (20 other events, 70.3 us)
Sparse Core Ops, SparseCore 0:
  82.1 69.3 reduce-scatter.4
  233.9 69.2 reduce-scatter.6
  385.4 69.2 reduce-scatter.8
  535.9 69.2 reduce-scatter.10
